TPU v7x, 32 devices: a whole 2x2x4 slice. The times are simulated.
32 devices in a mesh: clip: 2 (over y), xt: 4 (over z), tb: 2 (over x), luma: 2 (over core).
Axes of the slice: x: 2, y: 2, z: 4, core: 2. Of those that a mesh axis runs over, the one named last changes fastest.
Arguments:
- target: float32 [8, 2, 2, 4, 8, 8, 2, 128], P(('clip', 'xt'), 'tb', 'luma'), parts along dimension 0, may hold values from -1 to 6
- confidence: float32 [8, 2, 2, 4, 8, 8, 2, 128], P(('clip', 'xt'), 'tb', 'luma'), parts along dimension 0, may hold values from 0.05 to 1
- normalizer: float32 [8, 2, 2, 4, 8, 8, 2, 128], P(('clip', 'xt'), 'tb', 'luma'), parts along dimension 0, may hold values from 0.5 to 1
- brick_slots: int32 [8, 2, 2, 4], P(('clip', 'xt'), 'tb', 'luma'), parts along dimension 0, may hold values from 0 to 7, as said below
- brick_counts: int32 [8, 2, 2], P(('clip', 'xt'), 'tb', 'luma'), parts along dimension 0, may hold values from 1 to 4, as said below
Outputs:
- solution: float32 [8, 2, 2, 4, 8, 8, 2, 128], P(('clip', 'xt'), 'tb', 'luma'), parts along dimension 0
There are 2 independent parts, one for each index of `clip`. A program takes and returns all parts, laid end to end along the dimension named above; each array names one. Nothing has to cross between parts.
Inputs may be any that keep to these rules, and one draw needn't show every extreme that they name: `brick_slots`: in each device's list the 4 entries name different positions; position s is the brick (s // 4, (s // 2) % 2, s % 2) of the device's 2 x 2 x 2 region of time, luma and x bricks. The first brick_counts entries of a device's list are its occupied bricks; some device has 4.
All inputs are finite; a program needn't handle non-finite values.
Results may differ from a plain program's by a relative error of at most 0.0003.
Values sent between devices are 32-bit elements; how exact they have to be, the bound alone decides.
A program may use at most 64 MiB of HBM per device.

v0:
```python
import jax
import jax.numpy as jnp
from jax import lax
from jax.sharding import PartitionSpec as P

BT = 8
BL = 8
BX = 2
RT = 2
RL = 2
RX = 2
ITERS = 3
SLOTS = 8


smoothness = 8.0


def padded_2(array, sides, width):
    for axis, dim in sides:
        count, length = (lax.axis_size(axis), array.shape[dim])
        up = [(i, (i + 1) % count) for i in range(count - 1)]
        down = [(j, i) for i, j in up]
        last = lax.slice_in_dim(array, length - width, length, axis=dim)
        initial = lax.slice_in_dim(array, 0, width, axis=dim)
        before = lax.ppermute(last, axis, up)
        after = lax.ppermute(initial, axis, down)
        array = jnp.concatenate([before, array, after], axis=dim)
    return array


def smooth_axis(padded, axis):
    length = padded.shape[axis]
    first = lax.slice_in_dim(padded, 0, length - 2, axis=axis)
    middle = lax.slice_in_dim(padded, 1, length - 1, axis=axis)
    last = lax.slice_in_dim(padded, 2, length, axis=axis)
    return 0.25 * first + 0.5 * middle + 0.25 * last


def bilateral_smooth(region):
    padded = padded_2(region, (("xt", 2), ("tb", 0), ("luma", 1)), 1)
    padded = smooth_axis(padded, 0)
    padded = smooth_axis(padded, 1)
    padded = smooth_axis(padded, 2)
    padded = jnp.pad(padded, ((0, 0), (0, 0), (0, 0), (1, 1)))
    return smooth_axis(padded, 3)


def per_device(target, confidence, normalizer, brick_slots, brick_counts):
    listed = target.shape[3]
    cells_y = target.shape[7]
    inner = (BT, BL, BX, cells_y)
    occupied = jnp.arange(listed, dtype=jnp.int32) < brick_counts.reshape(())
    keep = occupied.astype(jnp.float32)[:, None, None, None, None]
    slots_flat = brick_slots.reshape(listed)
    places = jnp.where(occupied, slots_flat, SLOTS)
    readable = jnp.where(occupied, slots_flat, 0)

    def to_region(values):
        region = jnp.zeros((SLOTS + 1,) + inner, jnp.float32).at[places].set(values)[:SLOTS]
        region = region.reshape(RT, RL, RX, BT, BL, BX, cells_y).transpose(0, 3, 1, 4, 2, 5, 6)
        return region.reshape(RT * BT, RL * BL, RX * BX, cells_y)

    def to_bricks(region):
        region = region.reshape(RT, BT, RL, BL, RX, BX, cells_y).transpose(0, 2, 4, 1, 3, 5, 6)
        region = region.reshape((SLOTS,) + inner)
        return jnp.take(region, readable, axis=0) * keep

    tvals = target.reshape((listed,) + inner) * keep
    cvals = confidence.reshape((listed,) + inner) * keep
    nvals = normalizer.reshape((listed,) + inner) * keep
    diagonal = smoothness * nvals * to_bricks(bilateral_smooth(to_region(nvals))) + cvals
    inverse = keep / jnp.where(keep > 0, diagonal, 1.0)

    def operator_apply(values):
        spread = to_bricks(bilateral_smooth(to_region(nvals * values)))
        return diagonal * values - smoothness * nvals * spread

    residual = cvals * tvals
    sol = jnp.zeros_like(residual)
    precond_r = inverse * residual
    image_u = operator_apply(precond_r)
    for iteration in range(ITERS):
        gamma, delta = lax.psum(
            (jnp.sum(residual * precond_r), jnp.sum(image_u * precond_r)), ("xt", "tb", "luma")
        )
        if iteration + 1 < ITERS:
            precond_w = inverse * image_u
            image_pw = operator_apply(precond_w)
        if iteration == 0:
            alpha = gamma / delta
            direction = precond_r
        else:
            beta = gamma / gamma_prev
            alpha = gamma / (delta - beta * gamma / alpha_prev)
            direction = precond_r + beta * direction
        sol = sol + alpha * direction
        if iteration + 1 < ITERS:
            if iteration == 0:
                image_pdir = image_pw
                precond_dir = precond_w
                image_dir = image_u
            else:
                image_pdir = image_pw + beta * image_pdir
                precond_dir = precond_w + beta * precond_dir
                image_dir = image_u + beta * image_dir
            residual = residual - alpha * image_dir
            precond_r = precond_r - alpha * precond_dir
            image_u = image_u - alpha * image_pdir
        gamma_prev = gamma
        alpha_prev = alpha
    return sol.reshape(target.shape)


def solution(mesh):
    in_specs = (
        P(("clip", "xt"), "tb", "luma", None, None, None, None, None),
        P(("clip", "xt"), "tb", "luma", None, None, None, None, None),
        P(("clip", "xt"), "tb", "luma", None, None, None, None, None),
        P(("clip", "xt"), "tb", "luma", None),
        P(("clip", "xt"), "tb", "luma"),
    )
    out_specs = P(("clip", "xt"), "tb", "luma", None, None, None, None, None)
    return jax.shard_map(
        per_device, mesh=mesh, in_specs=in_specs, out_specs=out_specs, check_vma=False
    )
```

profile of v0, /device:TPU:0, one launch (start us, length us, event | category | flops | bytes accessed | tf_op | source)
XLA Modules:
  0.0 207.3 jit_solution(17528638098363374982)
XLA Ops:
  0.7 0.7 compare_and_fusion
  1.3 0.7 fusion.54
  2.0 1.0 bitcast_multiply_fusion
  3.1 0.7 scatter_fusion
  3.9 4.9 %collective-permute-start = (f32[16,16,1,128]{3,1,2,0:T(8,128)S(1)}, f32[16,16,1,128]{3,1,2,0:T(8,128)S(1)}, u32[]{:S(2)}, u32[]{:S(2)}) collective-permute-start(f32[16,16,1,128]{3,1,2,0:T(8,128)S(1)} %get-tuple-element.47), channel_id=1, source_target_pairs={{0,4},{4,8},{8,12},{1,5},{5,9},{9,13},{2,6},{6,10},{10,14},{3,7},{... | collective-permute-start | bytes 393224 | tf_op jit(solution)/shard_map/ppermute | solution.py:26
  8.8 1.3 collective-permute-start.1
  10.1 1.4 collective-permute-done
  11.5 4.1 %collective-permute-done.1 = f32[16,16,1,128]{3,1,2,0:T(8,128)S(1)} collective-permute-done((f32[16,16,1,128]{3,1,2,0:T(8,128)S(1)}, f32[16,16,1,128]{3,1,2,0:T(8,128)S(1)}, u32[]{:S(2)}, u32[]{:S(2)}) %collective-permute-start.1) | collective-permute-done | bytes 131104 | tf_op jit(solution)/shard_map/ppermute | solution.py:27
  15.7 3.4 %collective-permute-start.2 = (f32[1,16,6,128]{3,1,2,0:T(8,128)S(1)}, f32[1,16,6,128]{3,1,2,0:T(8,128)S(1)}, u32[]{:S(2)}, u32[]{:S(2)}) collective-permute-start(f32[1,16,6,128]{3,1,2,0:T(8,128)S(1)} %get-tuple-element.39), channel_id=1, source_target_pairs={{0,2},{1,3},{4,6},{5,7},{8,10},{9,11},{12,14},{13,15},{16,18},{17,... | collective-permute-start | bytes 147464 | tf_op jit(solution)/shard_map/ppermute | solution.py:26
  19.1 1.3 collective-permute-start.3
  20.4 0.4 collective-permute-done.2
  20.8 4.3 %collective-permute-done.3 = f32[1,16,6,128]{3,1,2,0:T(8,128)S(1)} collective-permute-done((f32[1,16,6,128]{3,1,2,0:T(8,128)S(1)}, f32[1,16,6,128]{3,1,2,0:T(8,128)S(1)}, u32[]{:S(2)}, u32[]{:S(2)}) %collective-permute-start.3) | collective-permute-done | bytes 49184 | tf_op jit(solution)/shard_map/ppermute | solution.py:27
  25.2 1.3 collective-permute-start.4
  26.5 1.3 collective-permute-start.5
  27.8 1.8 collective-permute-done.5
  30.3 0.3 fusion.18
  30.7 0.6 gather_fusion
  31.7 0.7 scatter_fusion.1
  32.5 3.5 %collective-permute-start.6 = (f32[16,16,1,128]{3,1,2,0:T(8,128)S(1)}, f32[16,16,1,128]{3,1,2,0:T(8,128)S(1)}, u32[]{:S(2)}, u32[]{:S(2)}) collective-permute-start(f32[16,16,1,128]{3,1,2,0:T(8,128)S(1)} %get-tuple-element.45), channel_id=1, source_target_pairs={{0,4},{4,8},{8,12},{1,5},{5,9},{9,13},{2,6},{6,10},{10,14},{3,7},{... | collective-permute-start | bytes 393224 | tf_op jit(solution)/shard_map/ppermute | solution.py:26
  36.0 1.3 collective-permute-start.7
  37.3 1.8 collective-permute-done.6
  39.0 4.1 %collective-permute-done.7 = f32[16,16,1,128]{3,1,2,0:T(8,128)S(1)} collective-permute-done((f32[16,16,1,128]{3,1,2,0:T(8,128)S(1)}, f32[16,16,1,128]{3,1,2,0:T(8,128)S(1)}, u32[]{:S(2)}, u32[]{:S(2)}) %collective-permute-start.7) | collective-permute-done | bytes 131104 | tf_op jit(solution)/shard_map/ppermute | solution.py:27
  43.2 1.6 collective-permute-start.8
  44.8 1.3 collective-permute-start.9
  46.1 0.4 collective-permute-done.8
  46.5 4.3 %collective-permute-done.9 = f32[1,16,6,128]{3,1,2,0:T(8,128)S(1)} collective-permute-done((f32[1,16,6,128]{3,1,2,0:T(8,128)S(1)}, f32[1,16,6,128]{3,1,2,0:T(8,128)S(1)}, u32[]{:S(2)}, u32[]{:S(2)}) %collective-permute-start.9) | collective-permute-done | bytes 49184 | tf_op jit(solution)/shard_map/ppermute | solution.py:27
  50.8 1.3 collective-permute-start.10
  52.1 1.3 collective-permute-start.11
  53.4 1.8 collective-permute-done.11
  56.0 0.3 fusion.22
  56.4 0.6 gather_fusion.1
  56.9 0.8 multiply_reduce_fusion.3
  58.0 0.7 scatter_fusion.2
  58.8 3.5 %collective-permute-start.12 = (f32[16,16,1,128]{3,1,2,0:T(8,128)S(1)}, f32[16,16,1,128]{3,1,2,0:T(8,128)S(1)}, u32[]{:S(2)}, u32[]{:S(2)}) collective-permute-start(f32[16,16,1,128]{3,1,2,0:T(8,128)S(1)} %get-tuple-element.43), channel_id=1, source_target_pairs={{0,4},{4,8},{8,12},{1,5},{5,9},{9,13},{2,6},{6,10},{10,14},{3,7},{... | collective-permute-start | bytes 393224 | tf_op jit(solution)/shard_map/ppermute | solution.py:26
  62.2 1.3 collective-permute-start.13
  63.5 1.8 collective-permute-done.12
  65.3 4.1 %collective-permute-done.13 = f32[16,16,1,128]{3,1,2,0:T(8,128)S(1)} collective-permute-done((f32[16,16,1,128]{3,1,2,0:T(8,128)S(1)}, f32[16,16,1,128]{3,1,2,0:T(8,128)S(1)}, u32[]{:S(2)}, u32[]{:S(2)}) %collective-permute-start.13) | collective-permute-done | bytes 131104 | tf_op jit(solution)/shard_map/ppermute | solution.py:27
  69.4 1.6 collective-permute-start.14
  71.0 1.3 collective-permute-start.15
  72.3 0.4 collective-permute-done.14
  72.8 4.3 %collective-permute-done.15 = f32[1,16,6,128]{3,1,2,0:T(8,128)S(1)} collective-permute-done((f32[1,16,6,128]{3,1,2,0:T(8,128)S(1)}, f32[1,16,6,128]{3,1,2,0:T(8,128)S(1)}, u32[]{:S(2)}, u32[]{:S(2)}) %collective-permute-start.15) | collective-permute-done | bytes 49184 | tf_op jit(solution)/shard_map/ppermute | solution.py:27
  77.1 1.3 collective-permute-start.16
  78.4 1.3 collective-permute-start.17
  79.7 31.3 %all-reduce.6 = (f32[]{:T(128)}, f32[]{:T(128)}) all-reduce(f32[]{:T(128)} %get-tuple-element.11, f32[]{:T(128)} %get-tuple-element.10), channel_id=1, replica_groups=mesh['clip'=2,'xt'=4,'tb'=2,'luma'=2] {'xt','tb','luma'}, use_global_device_ids=true, to_apply=%region_2.4 | all-reduce | flops 2 | bytes 16 | tf_op jit(solution)/shard_map/psum | solution.py:84
  113.0 0.3 fusion.26
  113.4 0.6 gather_fusion.2
  114.0 1.0 multiply_reduce_fusion.1
  115.0 0.7 scatter_fusion.3
  115.8 1.3 collective-permute-start.18
  117.1 1.3 collective-permute-start.19
  118.4 1.2 collective-permute-done.18
  119.6 4.4 %collective-permute-done.19 = f32[16,16,1,128]{3,1,2,0:T(8,128)S(1)} collective-permute-done((f32[16,16,1,128]{3,1,2,0:T(8,128)S(1)}, f32[16,16,1,128]{3,1,2,0:T(8,128)S(1)}, u32[]{:S(2)}, u32[]{:S(2)}) %collective-permute-start.19) | collective-permute-done | bytes 131104 | tf_op jit(solution)/shard_map/ppermute | solution.py:27
  124.0 1.3 collective-permute-start.20
  125.3 1.3 collective-permute-start.21
  126.6 0.4 collective-permute-done.20
  127.0 4.3 %collective-permute-done.21 = f32[1,16,6,128]{3,1,2,0:T(8,128)S(1)} collective-permute-done((f32[1,16,6,128]{3,1,2,0:T(8,128)S(1)}, f32[1,16,6,128]{3,1,2,0:T(8,128)S(1)}, u32[]{:S(2)}, u32[]{:S(2)}) %collective-permute-start.21) | collective-permute-done | bytes 49184 | tf_op jit(solution)/shard_map/ppermute | solution.py:27
  131.4 1.3 collective-permute-start.22
  132.7 1.3 collective-permute-start.23
  134.0 31.2 %all-reduce.5 = (f32[]{:T(128)}, f32[]{:T(128)}) all-reduce(f32[]{:T(128)} %get-tuple-element.9, f32[]{:T(128)} %get-tuple-element.8), channel_id=1, replica_groups=mesh['clip'=2,'xt'=4,'tb'=2,'luma'=2] {'xt','tb','luma'}, use_global_device_ids=true, to_apply=%region_7.9 | all-reduce | flops 2 | bytes 16 | tf_op jit(solution)/shard_map/psum | solution.py:84
  170.6 0.6 gather_fusion.3
  171.1 1.1 fusion.47
  172.2 30.1 %all-reduce.4 = (f32[]{:T(128)}, f32[]{:T(128)}) all-reduce(f32[]{:T(128)} %get-tuple-element.7, f32[]{:T(128)} %get-tuple-element.6), channel_id=1, replica_groups=mesh['clip'=2,'xt'=4,'tb'=2,'luma'=2] {'xt','tb','luma'}, use_global_device_ids=true, to_apply=%region_12.14 | all-reduce | flops 2 | bytes 16 | tf_op jit(solution)/shard_map/psum | solution.py:84
  206.1 0.3 add_bitcast_fusion
  206.5 0.8 copy.21
  (61 shorter events, 4.7 us)
Async XLA Ops:
  3.9 7.7 %collective-permute-start = (f32[16,16,1,128]{3,1,2,0:T(8,128)S(1)}, f32[16,16,1,128]{3,1,2,0:T(8,128)S(1)}, u32[]{:S(2)}, u32[]{:S(2)}) collective-permute-start(f32[16,16,1,128]{3,1,2,0:T(8,128)S(1)} %get-tuple-element.47), channel_id=1, source_target_pairs={{0,4},{4,8},{8,12},{1,5},{5,9},{9,13},{2,6},{6,10},{10,14},{3,7},{... | collective-permute-start | bytes 393224 | tf_op jit(solution)/shard_map/ppermute | solution.py:26
  8.8 6.9 %collective-permute-start.1 = (f32[16,16,1,128]{3,1,2,0:T(8,128)S(1)}, f32[16,16,1,128]{3,1,2,0:T(8,128)S(1)}, u32[]{:S(2)}, u32[]{:S(2)}) collective-permute-start(f32[16,16,1,128]{3,1,2,0:T(8,128)S(1)} %get-tuple-element.48), channel_id=1, source_target_pairs={{4,0},{8,4},{12,8},{5,1},{9,5},{13,9},{6,2},{10,6},{14,10},{7,3},{... | collective-permute-start | bytes 393224 | tf_op jit(solution)/shard_map/ppermute | solution.py:27
  15.7 5.1 %collective-permute-start.2 = (f32[1,16,6,128]{3,1,2,0:T(8,128)S(1)}, f32[1,16,6,128]{3,1,2,0:T(8,128)S(1)}, u32[]{:S(2)}, u32[]{:S(2)}) collective-permute-start(f32[1,16,6,128]{3,1,2,0:T(8,128)S(1)} %get-tuple-element.39), channel_id=1, source_target_pairs={{0,2},{1,3},{4,6},{5,7},{8,10},{9,11},{12,14},{13,15},{16,18},{17,... | collective-permute-start | bytes 147464 | tf_op jit(solution)/shard_map/ppermute | solution.py:26
  19.1 6.0 %collective-permute-start.3 = (f32[1,16,6,128]{3,1,2,0:T(8,128)S(1)}, f32[1,16,6,128]{3,1,2,0:T(8,128)S(1)}, u32[]{:S(2)}, u32[]{:S(2)}) collective-permute-start(f32[1,16,6,128]{3,1,2,0:T(8,128)S(1)} %get-tuple-element.40), channel_id=1, source_target_pairs={{2,0},{3,1},{6,4},{7,5},{10,8},{11,9},{14,12},{15,13},{18,16},{19,... | collective-permute-start | bytes 147464 | tf_op jit(solution)/shard_map/ppermute | solution.py:27
  25.2 2.6 %collective-permute-start.4 = (f32[18,1,6,128]{3,1,2,0:T(1,128)S(1)}, f32[18,1,6,128]{3,1,2,0:T(1,128)S(1)}, u32[]{:S(2)}, u32[]{:S(2)}) collective-permute-start(f32[18,1,6,128]{3,1,2,0:T(1,128)S(1)} %get-tuple-element.31), channel_id=1, source_target_pairs={{0,1},{2,3},{4,5},{6,7},{8,9},{10,11},{12,13},{14,15},{16,17},{18,... | collective-permute-start | bytes 165896 | tf_op jit(solution)/shard_map/ppermute | solution.py:26
  26.5 3.1 %collective-permute-start.5 = (f32[18,1,6,128]{3,1,2,0:T(1,128)S(1)}, f32[18,1,6,128]{3,1,2,0:T(1,128)S(1)}, u32[]{:S(2)}, u32[]{:S(2)}) collective-permute-start(f32[18,1,6,128]{3,1,2,0:T(1,128)S(1)} %get-tuple-element.32), channel_id=1, source_target_pairs={{1,0},{3,2},{5,4},{7,6},{9,8},{11,10},{13,12},{15,14},{17,16},{19,... | collective-permute-start | bytes 165896 | tf_op jit(solution)/shard_map/ppermute | solution.py:27
  30.3 1.0 copy-start
  30.3 1.0 copy-start.1
  30.3 1.1 copy-start.2
  32.5 6.5 %collective-permute-start.6 = (f32[16,16,1,128]{3,1,2,0:T(8,128)S(1)}, f32[16,16,1,128]{3,1,2,0:T(8,128)S(1)}, u32[]{:S(2)}, u32[]{:S(2)}) collective-permute-start(f32[16,16,1,128]{3,1,2,0:T(8,128)S(1)} %get-tuple-element.45), channel_id=1, source_target_pairs={{0,4},{4,8},{8,12},{1,5},{5,9},{9,13},{2,6},{6,10},{10,14},{3,7},{... | collective-permute-start | bytes 393224 | tf_op jit(solution)/shard_map/ppermute | solution.py:26
  36.0 7.2 %collective-permute-start.7 = (f32[16,16,1,128]{3,1,2,0:T(8,128)S(1)}, f32[16,16,1,128]{3,1,2,0:T(8,128)S(1)}, u32[]{:S(2)}, u32[]{:S(2)}) collective-permute-start(f32[16,16,1,128]{3,1,2,0:T(8,128)S(1)} %get-tuple-element.46), channel_id=1, source_target_pairs={{4,0},{8,4},{12,8},{5,1},{9,5},{13,9},{6,2},{10,6},{14,10},{7,3},{... | collective-permute-start | bytes 393224 | tf_op jit(solution)/shard_map/ppermute | solution.py:27
  43.2 3.3 %collective-permute-start.8 = (f32[1,16,6,128]{3,1,2,0:T(8,128)S(1)}, f32[1,16,6,128]{3,1,2,0:T(8,128)S(1)}, u32[]{:S(2)}, u32[]{:S(2)}) collective-permute-start(f32[1,16,6,128]{3,1,2,0:T(8,128)S(1)} %get-tuple-element.37), channel_id=1, source_target_pairs={{0,2},{1,3},{4,6},{5,7},{8,10},{9,11},{12,14},{13,15},{16,18},{17,... | collective-permute-start | bytes 147464 | tf_op jit(solution)/shard_map/ppermute | solution.py:26
  44.8 6.0 %collective-permute-start.9 = (f32[1,16,6,128]{3,1,2,0:T(8,128)S(1)}, f32[1,16,6,128]{3,1,2,0:T(8,128)S(1)}, u32[]{:S(2)}, u32[]{:S(2)}) collective-permute-start(f32[1,16,6,128]{3,1,2,0:T(8,128)S(1)} %get-tuple-element.38), channel_id=1, source_target_pairs={{2,0},{3,1},{6,4},{7,5},{10,8},{11,9},{14,12},{15,13},{18,16},{19,... | collective-permute-start | bytes 147464 | tf_op jit(solution)/shard_map/ppermute | solution.py:27
  50.8 2.6 %collective-permute-start.10 = (f32[18,1,6,128]{3,1,2,0:T(1,128)S(1)}, f32[18,1,6,128]{3,1,2,0:T(1,128)S(1)}, u32[]{:S(2)}, u32[]{:S(2)}) collective-permute-start(f32[18,1,6,128]{3,1,2,0:T(1,128)S(1)} %get-tuple-element.29), channel_id=1, source_target_pairs={{0,1},{2,3},{4,5},{6,7},{8,9},{10,11},{12,13},{14,15},{16,17},{18,... | collective-permute-start | bytes 165896 | tf_op jit(solution)/shard_map/ppermute | solution.py:26
  52.1 3.1 %collective-permute-start.11 = (f32[18,1,6,128]{3,1,2,0:T(1,128)S(1)}, f32[18,1,6,128]{3,1,2,0:T(1,128)S(1)}, u32[]{:S(2)}, u32[]{:S(2)}) collective-permute-start(f32[18,1,6,128]{3,1,2,0:T(1,128)S(1)} %get-tuple-element.30), channel_id=1, source_target_pairs={{1,0},{3,2},{5,4},{7,6},{9,8},{11,10},{13,12},{15,14},{17,16},{19,... | collective-permute-start | bytes 165896 | tf_op jit(solution)/shard_map/ppermute | solution.py:27
  58.8 6.5 %collective-permute-start.12 = (f32[16,16,1,128]{3,1,2,0:T(8,128)S(1)}, f32[16,16,1,128]{3,1,2,0:T(8,128)S(1)}, u32[]{:S(2)}, u32[]{:S(2)}) collective-permute-start(f32[16,16,1,128]{3,1,2,0:T(8,128)S(1)} %get-tuple-element.43), channel_id=1, source_target_pairs={{0,4},{4,8},{8,12},{1,5},{5,9},{9,13},{2,6},{6,10},{10,14},{3,7},{... | collective-permute-start | bytes 393224 | tf_op jit(solution)/shard_map/ppermute | solution.py:26
  62.2 7.2 %collective-permute-start.13 = (f32[16,16,1,128]{3,1,2,0:T(8,128)S(1)}, f32[16,16,1,128]{3,1,2,0:T(8,128)S(1)}, u32[]{:S(2)}, u32[]{:S(2)}) collective-permute-start(f32[16,16,1,128]{3,1,2,0:T(8,128)S(1)} %get-tuple-element.44), channel_id=1, source_target_pairs={{4,0},{8,4},{12,8},{5,1},{9,5},{13,9},{6,2},{10,6},{14,10},{7,3},{... | collective-permute-start | bytes 393224 | tf_op jit(solution)/shard_map/ppermute | solution.py:27
  69.4 3.3 %collective-permute-start.14 = (f32[1,16,6,128]{3,1,2,0:T(8,128)S(1)}, f32[1,16,6,128]{3,1,2,0:T(8,128)S(1)}, u32[]{:S(2)}, u32[]{:S(2)}) collective-permute-start(f32[1,16,6,128]{3,1,2,0:T(8,128)S(1)} %get-tuple-element.35), channel_id=1, source_target_pairs={{0,2},{1,3},{4,6},{5,7},{8,10},{9,11},{12,14},{13,15},{16,18},{17,... | collective-permute-start | bytes 147464 | tf_op jit(solution)/shard_map/ppermute | solution.py:26
  71.0 6.0 %collective-permute-start.15 = (f32[1,16,6,128]{3,1,2,0:T(8,128)S(1)}, f32[1,16,6,128]{3,1,2,0:T(8,128)S(1)}, u32[]{:S(2)}, u32[]{:S(2)}) collective-permute-start(f32[1,16,6,128]{3,1,2,0:T(8,128)S(1)} %get-tuple-element.36), channel_id=1, source_target_pairs={{2,0},{3,1},{6,4},{7,5},{10,8},{11,9},{14,12},{15,13},{18,16},{19,... | collective-permute-start | bytes 147464 | tf_op jit(solution)/shard_map/ppermute | solution.py:27
  77.1 35.2 %collective-permute-start.16 = (f32[18,1,6,128]{3,1,2,0:T(1,128)S(1)}, f32[18,1,6,128]{3,1,2,0:T(1,128)S(1)}, u32[]{:S(2)}, u32[]{:S(2)}) collective-permute-start(f32[18,1,6,128]{3,1,2,0:T(1,128)S(1)} %get-tuple-element.27), channel_id=1, source_target_pairs={{0,1},{2,3},{4,5},{6,7},{8,9},{10,11},{12,13},{14,15},{16,17},{18,... | collective-permute-start | bytes 165896 | tf_op jit(solution)/shard_map/ppermute | solution.py:26
  78.4 33.9 %collective-permute-start.17 = (f32[18,1,6,128]{3,1,2,0:T(1,128)S(1)}, f32[18,1,6,128]{3,1,2,0:T(1,128)S(1)}, u32[]{:S(2)}, u32[]{:S(2)}) collective-permute-start(f32[18,1,6,128]{3,1,2,0:T(1,128)S(1)} %get-tuple-element.28), channel_id=1, source_target_pairs={{1,0},{3,2},{5,4},{7,6},{9,8},{11,10},{13,12},{15,14},{17,16},{19,... | collective-permute-start | bytes 165896 | tf_op jit(solution)/shard_map/ppermute | solution.py:27
  115.8 3.8 %collective-permute-start.18 = (f32[16,16,1,128]{3,1,2,0:T(8,128)S(1)}, f32[16,16,1,128]{3,1,2,0:T(8,128)S(1)}, u32[]{:S(2)}, u32[]{:S(2)}) collective-permute-start(f32[16,16,1,128]{3,1,2,0:T(8,128)S(1)} %get-tuple-element.41), channel_id=1, source_target_pairs={{0,4},{4,8},{8,12},{1,5},{5,9},{9,13},{2,6},{6,10},{10,14},{3,7},{... | collective-permute-start | bytes 393224 | tf_op jit(solution)/shard_map/ppermute | solution.py:26
  117.1 6.9 %collective-permute-start.19 = (f32[16,16,1,128]{3,1,2,0:T(8,128)S(1)}, f32[16,16,1,128]{3,1,2,0:T(8,128)S(1)}, u32[]{:S(2)}, u32[]{:S(2)}) collective-permute-start(f32[16,16,1,128]{3,1,2,0:T(8,128)S(1)} %get-tuple-element.42), channel_id=1, source_target_pairs={{4,0},{8,4},{12,8},{5,1},{9,5},{13,9},{6,2},{10,6},{14,10},{7,3},{... | collective-permute-start | bytes 393224 | tf_op jit(solution)/shard_map/ppermute | solution.py:27
  124.0 3.0 %collective-permute-start.20 = (f32[1,16,6,128]{3,1,2,0:T(8,128)S(1)}, f32[1,16,6,128]{3,1,2,0:T(8,128)S(1)}, u32[]{:S(2)}, u32[]{:S(2)}) collective-permute-start(f32[1,16,6,128]{3,1,2,0:T(8,128)S(1)} %get-tuple-element.33), channel_id=1, source_target_pairs={{0,2},{1,3},{4,6},{5,7},{8,10},{9,11},{12,14},{13,15},{16,18},{17,... | collective-permute-start | bytes 147464 | tf_op jit(solution)/shard_map/ppermute | solution.py:26
  125.3 6.0 %collective-permute-start.21 = (f32[1,16,6,128]{3,1,2,0:T(8,128)S(1)}, f32[1,16,6,128]{3,1,2,0:T(8,128)S(1)}, u32[]{:S(2)}, u32[]{:S(2)}) collective-permute-start(f32[1,16,6,128]{3,1,2,0:T(8,128)S(1)} %get-tuple-element.34), channel_id=1, source_target_pairs={{2,0},{3,1},{6,4},{7,5},{10,8},{11,9},{14,12},{15,13},{18,16},{19,... | collective-permute-start | bytes 147464 | tf_op jit(solution)/shard_map/ppermute | solution.py:27
  131.4 38.1 %collective-permute-start.22 = (f32[18,1,6,128]{3,1,2,0:T(1,128)S(1)}, f32[18,1,6,128]{3,1,2,0:T(1,128)S(1)}, u32[]{:S(2)}, u32[]{:S(2)}) collective-permute-start(f32[18,1,6,128]{3,1,2,0:T(1,128)S(1)} %get-tuple-element.25), channel_id=1, source_target_pairs={{0,1},{2,3},{4,5},{6,7},{8,9},{10,11},{12,13},{14,15},{16,17},{18,... | collective-permute-start | bytes 165896 | tf_op jit(solution)/shard_map/ppermute | solution.py:26
  132.7 36.8 %collective-permute-start.23 = (f32[18,1,6,128]{3,1,2,0:T(1,128)S(1)}, f32[18,1,6,128]{3,1,2,0:T(1,128)S(1)}, u32[]{:S(2)}, u32[]{:S(2)}) collective-permute-start(f32[18,1,6,128]{3,1,2,0:T(1,128)S(1)} %get-tuple-element.26), channel_id=1, source_target_pairs={{1,0},{3,2},{5,4},{7,6},{9,8},{11,10},{13,12},{15,14},{17,16},{19,... | collective-permute-start | bytes 165896 | tf_op jit(solution)/shard_map/ppermute | solution.py:27
where the time goes:
time: 208 us; the launch traced here: 207 us
  blocking collectives  92.6 us (45%)
  waiting for transfers between devices  45.2 us (22%)
  starting transfers between devices  41.8 us (20%)
  between operations  10.8 us (5%)
  other arithmetic  10.4 us (5%)
  local copies, waits for them, and re-layouts  6.63 us (3%)
    psum x3, blocking collectives, per_device(): lax.psum((jnp.sum(residual * precond_r), jnp.sum(image_u * precond_r)), (...  92.6 us
    ppermute x12, waiting for transfers between devices, padded_2(): after = lax.ppermute(initial, axis, down)  37.4 us
    ppermute x12, starting transfers between devices, padded_2(): before = lax.ppermute(last, axis, up)  26.3 us
    ppermute x12, starting transfers between devices, padded_2(): after = lax.ppermute(initial, axis, down)  15.5 us
    ppermute x12, waiting for transfers between devices, padded_2(): before = lax.ppermute(last, axis, up)  7.86 us
  transfers between devices with their start and end apart: 24, of which 18 were waited for; matrix products, arithmetic and copies ran while one was open for 0% of the time, Pallas kernels for 0%

commit v1 on v0

v1 whole, which is shorter than its diff:
```python
import functools

import jax
import jax.numpy as jnp
from jax import lax
from jax.experimental import pallas as pl
from jax.experimental.pallas import tpu as pltpu
from jax.sharding import PartitionSpec as P

MESH = pl.DeviceIdType.MESH
SHIFT = 0.5
STAGES = 4
SIDES = (-1, 0, 1)
MESSAGES = [(dx, dt, dl) for dl in (0, 1) for dx in SIDES for dt in SIDES if (dx, dt, dl) != (0, 0, 0)]
NEAR = [m for m in MESSAGES if m[0] == 0]
FAR = [m for m in MESSAGES if m[0] != 0]


def kernel(
    nx, nt,
    slots, counts, target, confidence, normalizer, out,
    tin, cin, nin, bricks, n_, c_, r_, d_, m_, p0_, p1_, p2_, u0_,
    q_, es, er, fs, ff, acc, gathered,
    in_sem, send_sem, recv_sem, sum_send, sum_recv,
):
    ix, it, il = lax.axis_index("xt"), lax.axis_index("tb"), lax.axis_index("luma")
    peers = nx * nt * 2
    me = (ix * nt + it) * 2 + il

    loads = [
        pltpu.make_async_copy(src, dst, in_sem.at[i])
        for i, (src, dst) in enumerate(((normalizer, nin), (confidence, cin), (target, tin)))
    ]
    for load in loads:
        load.start()

    @pl.when(ix == 0)
    def _():
        q_[:, 0] = jnp.zeros_like(q_[:, 0])
        er[:, 0] = jnp.zeros_like(er[:, 0])

    @pl.when(ix == nx - 1)
    def _():
        q_[:, 5] = jnp.zeros_like(q_[:, 5])
        er[:, 5] = jnp.zeros_like(er[:, 5])

    @pl.when(it == 0)
    def _():
        q_[:, :, 0] = jnp.zeros_like(q_[:, :, 0])
        er[:, :, 0:8] = jnp.zeros_like(er[:, :, 0:8])

    @pl.when(it == nt - 1)
    def _():
        q_[:, :, 17] = jnp.zeros_like(q_[:, :, 17])
        er[:, :, 24:32] = jnp.zeros_like(er[:, :, 24:32])

    def peer_id(r):
        other = lax.rem(me + r, peers)
        return {"xt": lax.div(other, 2 * nt), "tb": lax.rem(lax.div(other, 2), nt), "luma": lax.rem(other, 2)}

    def each_peer(act):
        if peers <= 16:
            for r in range(1, peers):
                act(r)
        else:
            def step(r, carry):
                act(r)
                return carry
            lax.fori_loop(1, peers, step, 0)

    barrier = pltpu.get_barrier_semaphore()
    each_peer(lambda r: pl.semaphore_signal(barrier, inc=1, device_id=peer_id(r), device_id_type=MESH))

    row = lax.broadcasted_iota(jnp.int32, (16, 128), 0)
    col = lax.broadcasted_iota(jnp.int32, (16, 128), 1)
    edge = jnp.where(row == jnp.where(il == 0, 15, 0), 1.0, 0.0).astype(jnp.float32)
    zero = jnp.zeros((16, 128), jnp.float32)

    entry, here = [], []
    for s in range(8):
        k_s, h_s = jnp.int32(0), jnp.float32(0.0)
        for k in range(4):
            hit = jnp.logical_and(slots[0, 0, 0, k] == s, k < counts[0, 0, 0])
            k_s = jnp.where(hit, k, k_s)
            h_s = jnp.where(hit, 1.0, h_s)
        entry.append(k_s)
        here.append(h_s)

    def place(source, body):
        def step(i, carry):
            for s in range(8):
                bricks[s, i] = source[entry[s], i] * here[s]
            for s in range(8):
                rt, rl, rx = s // 4, (s // 2) % 2, s % 2
                for lx in range(2):
                    values = bricks[s, i, pl.ds(lx, 8, stride=2), :]
                    body(values, (rx * 2 + lx, rt * 8 + i, pl.ds(rl * 8, 8)))
            return carry
        lax.fori_loop(0, 8, step, 0)

    def emit(stage, x, t, values):
        tile = (
            2.0 * values
            + jnp.where(col == 0, 0.0, pltpu.roll(values, 1, 1))
            + jnp.where(col == 127, 0.0, pltpu.roll(values, 127, 1))
        )
        q_[stage, x + 1, t + 1] = tile
        es[stage, x, pl.ds(t, 1), :] = jnp.where(il == 0, tile[15:16], tile[0:1])

    def message(stage, which):
        dx, dt, dl = which
        i = MESSAGES.index(which)
        to = {"xt": ix + dx, "tb": it + dt, "luma": 1 - il if dl else il}
        if dl == 0:
            xs = {1: (4, 0), -1: (1, 5), 0: (pl.ds(1, 4), pl.ds(1, 4))}[dx]
            ts = {1: (16, 0), -1: (1, 17), 0: (pl.ds(1, 16), pl.ds(1, 16))}[dt]
            src, dst = (q_.at[stage, xs[j], ts[j]] for j in (0, 1))
        else:
            xs = {1: (3, 0), -1: (0, 5), 0: (pl.ds(0, 4), pl.ds(1, 4))}[dx]
            ts = {
                1: (pl.ds(8, 8), pl.ds(0, 8)),
                -1: (pl.ds(0, 8), pl.ds(24, 8)),
                0: (pl.ds(0, 16), pl.ds(8, 16)),
            }[dt]
            src, dst = es.at[stage, xs[0], ts[0]], er.at[stage, xs[1], ts[1]]
        return pltpu.make_async_remote_copy(
            src_ref=src, dst_ref=dst, send_sem=send_sem.at[stage, i], recv_sem=recv_sem.at[stage, i],
            device_id=to, device_id_type=MESH,
        )

    def guarded(which, sign, act):
        dx, dt, _ = which
        conds = []
        for d, at, size in ((dx * sign, ix, nx), (dt * sign, it, nt)):
            if d == 1:
                conds.append(at < size - 1)
            elif d == -1:
                conds.append(at > 0)
        if conds:
            pl.when(functools.reduce(jnp.logical_and, conds))(act)
        else:
            act()

    def send(stage, group):
        for which in group:
            guarded(which, 1, lambda which=which: message(stage, which).start())

    def receive(stage, group):
        for which in group:
            guarded(which, -1, lambda which=which: message(stage, which).wait_recv())

    def spread(stage, xs, update, carry):
        for x in xs:
            g = er[stage, x] + 2.0 * er[stage, x + 1] + er[stage, x + 2]
            fs[x] = g
            ff[x] = fs[x, pl.ds(7, 16)] + 2.0 * fs[x, pl.ds(8, 16)] + fs[x, pl.ds(9, 16)]
        need = sorted({x + d for x in xs for d in (0, 1, 2)})

        def step(t, carry):
            sums = {
                x: q_[stage, x, t] + 2.0 * q_[stage, x, t + 1] + q_[stage, x, t + 2] for x in need
            }
            for x in xs:
                a = sums[x] + 2.0 * sums[x + 1] + sums[x + 2]
                smoothed = (
                    2.0 * a
                    + jnp.where(row == 0, 0.0, pltpu.roll(a, 1, 0))
                    + jnp.where(row == 15, 0.0, pltpu.roll(a, 15, 0))
                    + edge * ff[x, pl.ds(t, 1), :]
                )
                carry = update(x, t, smoothed, carry)
            return carry

        return lax.fori_loop(0, 16, step, carry)

    def keep_sum(i, total):
        acc[pl.ds(i, 1), :] = jnp.sum(total, axis=0, keepdims=True)

    loads[0].wait()

    def put_n(values, at):
        n_[at] = values

    place(nin, put_n)

    def first(t, carry):
        for x in range(4):
            emit(0, x, t, n_[x, t])
        return carry

    lax.fori_loop(0, 16, first, 0)
    pl.semaphore_wait(barrier, peers - 1)
    send(0, FAR)
    send(0, NEAR)

    loads[1].wait()
    loads[2].wait()

    def put_c(values, at):
        c_[at] = values

    def put_r(values, at):
        r_[at] = c_[at] * values

    place(cin, put_c)
    place(tin, put_r)
    acc[...] = jnp.zeros((8, 128), jnp.float32)

    def update0(x, t, smoothed, carry):
        n = n_[x, t]
        diag = n * smoothed * (1.0 / 32.0) + c_[x, t]
        inverse = jnp.where(diag > 0.0, 1.0 / jnp.where(diag > 0.0, diag, 1.0), 0.0)
        r = r_[x, t]
        p = inverse * r
        d_[x, t] = diag
        m_[x, t] = inverse
        p0_[x, t] = p
        emit(1, x, t, n * p)
        return (carry[0] + r * p,)

    def image(p_ref, x, t, smoothed):
        p, n = p_ref[x, t], n_[x, t]
        return p, n, d_[x, t] * p - n * smoothed * (1.0 / 32.0)

    def update1(x, t, smoothed, carry):
        p, n, u = image(p0_, x, t, smoothed)
        later = m_[x, t] * u - SHIFT * p
        u0_[x, t] = u
        p1_[x, t] = later
        emit(2, x, t, n * later)
        return carry[0] + u * p, carry[1] + u * later

    def update2(x, t, smoothed, carry):
        p, n, u = image(p1_, x, t, smoothed)
        later = m_[x, t] * u - SHIFT * p
        p2_[x, t] = later
        emit(3, x, t, n * later)
        return carry[0] + u * p, carry[1] + u0_[x, t] * later, carry[2] + u * later

    def update3(x, t, smoothed, carry):
        p, n, u = image(p2_, x, t, smoothed)
        return (carry[0] + u * p,)

    rows = 0
    for stage, (update, count) in enumerate(((update0, 1), (update1, 2), (update2, 3), (update3, 1))):
        receive(stage, NEAR)
        carry = spread(stage, (1, 2), update, (zero,) * count)
        receive(stage, FAR)
        carry = spread(stage, (0, 3), update, carry)
        if stage + 1 < STAGES:
            send(stage + 1, FAR)
            send(stage + 1, NEAR)
        for total in carry:
            keep_sum(rows, total)
            rows += 1

    each_peer(
        lambda r: pltpu.make_async_remote_copy(
            src_ref=acc, dst_ref=gathered.at[r - 1], send_sem=sum_send, recv_sem=sum_recv,
            device_id=peer_id(r), device_id_type=MESH,
        ).start()
    )
    pltpu.make_async_copy(gathered, gathered, sum_recv).wait()
    total = acc[...] + jnp.sum(gathered[...], axis=0)
    total = jnp.sum(total, axis=1, keepdims=True)
    b0, g00, g01, g11, g02, g12, g22 = (total[i : i + 1] for i in range(7))
    b1 = g00 - SHIFT * b0
    b2 = g01 - SHIFT * b1
    l10, l20 = g01 / g00, g02 / g00
    d1 = g11 - l10 * g01
    e12 = g12 - l20 * g01
    l21 = e12 / d1
    d2 = g22 - l20 * g02 - l21 * e12
    y1 = b1 - l10 * b0
    y2 = b2 - l20 * b0 - l21 * y1
    x2 = y2 / d2
    x1 = y1 / d1 - l21 * x2
    x0 = b0 / g00 - l10 * x1 - l20 * x2
    w0, w1, w2 = (jnp.broadcast_to(v, (8, 128)) for v in (x0, x1, x2))

    def combine(i, carry):
        for s in range(8):
            rt, rl, rx = s // 4, (s // 2) % 2, s % 2
            for lx in range(2):
                at = (rx * 2 + lx, rt * 8 + i, pl.ds(rl * 8, 8))
                bricks[s, i, pl.ds(lx, 8, stride=2), :] = w0 * p0_[at] + w1 * p1_[at] + w2 * p2_[at]
        for k in range(4):
            out[k, i] = bricks[slots[0, 0, 0, k], i] * kept[k]
        return carry

    kept = [jnp.where(k < counts[0, 0, 0], 1.0, 0.0) for k in range(4)]
    lax.fori_loop(0, 8, combine, 0)

    for stage in range(STAGES):
        for which in MESSAGES:
            guarded(which, 1, lambda which=which: message(stage, which).wait_send())
    pltpu.make_async_copy(gathered, gathered, sum_send).wait()


def per_device(nx, nt, target, confidence, normalizer, brick_slots, brick_counts):
    shape = (4, 8, 16, 128)
    whole = (4, 16, 16, 128)
    peers = nx * nt * 2
    vmem = lambda *dims: pltpu.VMEM(dims, jnp.float32)
    smem = pl.BlockSpec(memory_space=pltpu.SMEM)
    anywhere = pl.BlockSpec(memory_space=pl.ANY)
    out = pl.pallas_call(
        functools.partial(kernel, nx, nt),
        out_shape=jax.ShapeDtypeStruct(shape, jnp.float32),
        in_specs=[smem, smem, anywhere, anywhere, anywhere],
        out_specs=pl.BlockSpec(memory_space=pltpu.VMEM),
        scratch_shapes=[vmem(*shape)] * 3
        + [vmem(8, 8, 16, 128)]
        + [vmem(*whole)] * 9
        + [
            vmem(STAGES, 6, 18, 16, 128),
            vmem(STAGES, 4, 16, 128),
            vmem(STAGES, 6, 32, 128),
            vmem(4, 32, 128),
            vmem(4, 16, 128),
            vmem(8, 128),
            vmem(peers - 1, 8, 128),
            pltpu.SemaphoreType.DMA((3,)),
            pltpu.SemaphoreType.DMA((STAGES, len(MESSAGES))),
            pltpu.SemaphoreType.DMA((STAGES, len(MESSAGES))),
            pltpu.SemaphoreType.DMA,
            pltpu.SemaphoreType.DMA,
        ],
        compiler_params=pltpu.CompilerParams(
            collective_id=0, has_side_effects=True, vmem_limit_bytes=32 * 1024 * 1024
        ),
    )(
        brick_slots, brick_counts,
        target.reshape(shape), confidence.reshape(shape), normalizer.reshape(shape),
    )
    return out.reshape(target.shape)


def solution(mesh):
    split = P(("clip", "xt"), "tb", "luma", None, None, None, None, None)
    in_specs = (
        split,
        split,
        split,
        P(("clip", "xt"), "tb", "luma", None),
        P(("clip", "xt"), "tb", "luma"),
    )
    return jax.shard_map(
        functools.partial(per_device, mesh.shape["xt"], mesh.shape["tb"]),
        mesh=mesh, in_specs=in_specs, out_specs=split, check_vma=False,
    )
```

time: 208 us -> 44.3 us (0.21)
  blocking collectives: 92.6 us -> 0 us
  waiting for transfers between devices: 45.2 us -> 0 us
  starting transfers between devices: 41.8 us -> 0 us
  Pallas kernels: 0 us -> 39.2 us
  other arithmetic: 10.4 us -> 0 us
  between operations: 10.8 us -> 0.67 us
  local copies, waits for them, and re-layouts: 6.63 us -> 4.2 us
    psum x3 -> x0, blocking collectives: 92.6 us -> none  [per_device(): lax.psum((jnp.sum(residual * precond_r), jnp.sum(image_u * precond_r)), (...]
    ppermute x24 -> x0, waiting for transfers between devices: 45.2 us -> none  [the longest x12 37.4 us: padded_2(): after = lax.ppermute(initial, axis, down)]
    ppermute x24 -> x0, starting transfers between devices: 41.8 us -> none  [the longest x12 26.3 us: padded_2(): before = lax.ppermute(last, axis, up)]
    pallas_call x0 -> x1, Pallas kernels: none -> 39.2 us  [per_device(): pl.pallas_call(functools.partial(kernel, nx, nt), out_shape=jax.ShapeDtyp...]
    unnamed x6 -> x9, local copies, waits for them, and re-layouts: 0.12 us -> 4.2 us
    add x16 -> x0, other arithmetic: 3.28 us -> none  [smooth_axis(): return 0.25 * first + 0.5 * middle + 0.25 * last]
    reduce_sum x3 -> x0, other arithmetic: 2.88 us -> none  [per_device(): jnp.sum(image_u * precond_r)]
    scatter x4 -> x0, local copies, waits for them, and re-layouts: 2.63 us -> none  [to_region(): jnp.zeros((SLOTS + 1,) + inner, jnp.float32).at[places].set(values)[:SLOTS]]
  transfers between devices with their start and end apart: 24 -> 0, of which waited for: 18 -> 0; matrix products, arithmetic and copies ran while one was open for 0% -> 0% of each run, Pallas kernels for 0% -> 0%
where the time goes in v1:
time: 44.3 us; the launch traced here: 44.1 us
  Pallas kernels  39.2 us (88%)
  local copies, waits for them, and re-layouts  4.2 us (9%)
  between operations  0.67 us (2%)
    pallas_call x1, Pallas kernels, per_device(): pl.pallas_call(functools.partial(kernel, nx, nt), out_shape=jax.ShapeDtyp...  39.2 us
    unnamed x9, local copies, waits for them, and re-layouts  4.2 us

profile of v1, /device:TPU:0, one launch (start us, length us, event | category | flops | bytes accessed | tf_op | source)
XLA Modules:
  0.0 44.1 jit_solution(289556602041584275)
XLA Ops:
  0.7 0.0 copy-start.3
  0.7 0.6 %copy-done.3 = s32[1,1,1,4]{3,2,1,0:T(1,128)S(1)} copy-done((s32[1,1,1,4]{3,2,1,0:T(1,128)S(1)}, s32[1,1,1,4]{3,2,1,0:T(1,128)}, u32[]{:S(2)}) %copy-start.3) | copy-done | bytes 40
  1.3 0.0 copy-start
  1.3 0.9 %copy-done = f32[1,1,1,4,8,8,2,128]{7,6,5,4,3,2,1,0:T(2,128)S(1)} copy-done((f32[1,1,1,4,8,8,2,128]{7,6,5,4,3,2,1,0:T(2,128)S(1)}, f32[1,1,1,4,8,8,2,128]{7,6,5,4,3,2,1,0:T(2,128)}, u32[]{:S(2)}) %copy-start) | copy-done | bytes 262168
  2.3 0.0 copy-start.1
  2.3 0.9 %copy-done.1 = f32[1,1,1,4,8,8,2,128]{7,6,5,4,3,2,1,0:T(2,128)S(1)} copy-done((f32[1,1,1,4,8,8,2,128]{7,6,5,4,3,2,1,0:T(2,128)S(1)}, f32[1,1,1,4,8,8,2,128]{7,6,5,4,3,2,1,0:T(2,128)}, u32[]{:S(2)}) %copy-start.1) | copy-done | bytes 262168
  3.2 0.0 copy-start.2
  3.2 0.9 %copy-done.2 = f32[1,1,1,4,8,8,2,128]{7,6,5,4,3,2,1,0:T(2,128)S(1)} copy-done((f32[1,1,1,4,8,8,2,128]{7,6,5,4,3,2,1,0:T(2,128)S(1)}, f32[1,1,1,4,8,8,2,128]{7,6,5,4,3,2,1,0:T(2,128)}, u32[]{:S(2)}) %copy-start.2) | copy-done | bytes 262168
  4.2 39.2 %shard_map.55 = f32[4,8,16,128]{3,2,1,0:T(8,128)S(1)} custom-call(s32[1,1,1,4]{3,2,1,0:T(1,128)S(1)} %copy-done.3, s32[1,1,1]{2,1,0:T(1,128)S(6)} %copy.7.counts, f32[4,8,16,128]{3,2,1,0:T(8,128)S(1)} %bitcast.5, f32[4,8,16,128]{3,2,1,0:T(8,128)S(1)} %bitcast.6, f32[4,8,16,128]{3,2,1,0:T(8,128)S(1)} %bitcast.7), custom_call_target="tpu_custom_call" | custom-call | tf_op jit(solution)/shard_map/pallas_call | solution.py:307
  43.4 0.7 %copy.8 = f32[1,1,1,4,8,8,2,128]{7,6,5,4,3,2,1,0:T(2,128)} copy(f32[1,1,1,4,8,8,2,128]{7,6,5,4,3,2,1,0:T(2,128)S(1)} %bitcast.4) | data formatting | bytes 524288
Async XLA Ops:
  0.7 0.7 %copy-start.3 = (s32[1,1,1,4]{3,2,1,0:T(1,128)S(1)}, s32[1,1,1,4]{3,2,1,0:T(1,128)}, u32[]{:S(2)}) copy-start(s32[1,1,1,4]{3,2,1,0:T(1,128)} %slots.1) | copy-start | bytes 52
  1.3 0.9 %copy-start = (f32[1,1,1,4,8,8,2,128]{7,6,5,4,3,2,1,0:T(2,128)S(1)}, f32[1,1,1,4,8,8,2,128]{7,6,5,4,3,2,1,0:T(2,128)}, u32[]{:S(2)}) copy-start(f32[1,1,1,4,8,8,2,128]{7,6,5,4,3,2,1,0:T(2,128)} %param.5) | copy-start | bytes 786436
  2.3 0.9 %copy-start.1 = (f32[1,1,1,4,8,8,2,128]{7,6,5,4,3,2,1,0:T(2,128)S(1)}, f32[1,1,1,4,8,8,2,128]{7,6,5,4,3,2,1,0:T(2,128)}, u32[]{:S(2)}) copy-start(f32[1,1,1,4,8,8,2,128]{7,6,5,4,3,2,1,0:T(2,128)} %param.6) | copy-start | bytes 786436
  3.2 0.9 %copy-start.2 = (f32[1,1,1,4,8,8,2,128]{7,6,5,4,3,2,1,0:T(2,128)S(1)}, f32[1,1,1,4,8,8,2,128]{7,6,5,4,3,2,1,0:T(2,128)}, u32[]{:S(2)}) copy-start(f32[1,1,1,4,8,8,2,128]{7,6,5,4,3,2,1,0:T(2,128)} %param.7) | copy-start | bytes 786436

commit v2 on v1

--- a/solution.py
+++ b/solution.py
@@ -10,6 +10,7 @@
 MESH = pl.DeviceIdType.MESH
 SHIFT = 0.5
 STAGES = 4
+UNROLL = 4
 SIDES = (-1, 0, 1)
 MESSAGES = [(dx, dt, dl) for dl in (0, 1) for dx in SIDES for dt in SIDES if (dx, dt, dl) != (0, 0, 0)]
 NEAR = [m for m in MESSAGES if m[0] == 0]
@@ -20,10 +21,11 @@
     nx, nt,
     slots, counts, target, confidence, normalizer, out,
     tin, cin, nin, bricks, n_, c_, r_, d_, m_, p0_, p1_, p2_, u0_,
-    q_, es, er, fs, ff, acc, gathered,
+    q0, q1, q2, q3, es0, es1, es2, es3, er0, er1, er2, er3, fs, ff, acc, gathered,
     in_sem, send_sem, recv_sem, sum_send, sum_recv,
 ):
     ix, it, il = lax.axis_index("xt"), lax.axis_index("tb"), lax.axis_index("luma")
+    q_, es, er = (q0, q1, q2, q3), (es0, es1, es2, es3), (er0, er1, er2, er3)
     peers = nx * nt * 2
     me = (ix * nt + it) * 2 + il
 
@@ -36,23 +38,27 @@
 
     @pl.when(ix == 0)
     def _():
-        q_[:, 0] = jnp.zeros_like(q_[:, 0])
-        er[:, 0] = jnp.zeros_like(er[:, 0])
+        for q, e in zip(q_, er):
+            q[0] = jnp.zeros_like(q[0])
+            e[0] = jnp.zeros_like(e[0])
 
     @pl.when(ix == nx - 1)
     def _():
-        q_[:, 5] = jnp.zeros_like(q_[:, 5])
-        er[:, 5] = jnp.zeros_like(er[:, 5])
+        for q, e in zip(q_, er):
+            q[5] = jnp.zeros_like(q[5])
+            e[5] = jnp.zeros_like(e[5])
 
     @pl.when(it == 0)
     def _():
-        q_[:, :, 0] = jnp.zeros_like(q_[:, :, 0])
-        er[:, :, 0:8] = jnp.zeros_like(er[:, :, 0:8])
+        for q, e in zip(q_, er):
+            q[:, 0] = jnp.zeros_like(q[:, 0])
+            e[:, 0:8] = jnp.zeros_like(e[:, 0:8])
 
     @pl.when(it == nt - 1)
     def _():
-        q_[:, :, 17] = jnp.zeros_like(q_[:, :, 17])
-        er[:, :, 24:32] = jnp.zeros_like(er[:, :, 24:32])
+        for q, e in zip(q_, er):
+            q[:, 17] = jnp.zeros_like(q[:, 17])
+            e[:, 24:32] = jnp.zeros_like(e[:, 24:32])
 
     def peer_id(r):
         other = lax.rem(me + r, peers)
@@ -104,8 +110,8 @@
             + jnp.where(col == 0, 0.0, pltpu.roll(values, 1, 1))
             + jnp.where(col == 127, 0.0, pltpu.roll(values, 127, 1))
         )
-        q_[stage, x + 1, t + 1] = tile
-        es[stage, x, pl.ds(t, 1), :] = jnp.where(il == 0, tile[15:16], tile[0:1])
+        q_[stage][x + 1, t + 1] = tile
+        es[stage][x, pl.ds(t, 1), :] = jnp.where(il == 0, tile[15:16], tile[0:1])
 
     def message(stage, which):
         dx, dt, dl = which
@@ -114,7 +120,7 @@
         if dl == 0:
             xs = {1: (4, 0), -1: (1, 5), 0: (pl.ds(1, 4), pl.ds(1, 4))}[dx]
             ts = {1: (16, 0), -1: (1, 17), 0: (pl.ds(1, 16), pl.ds(1, 16))}[dt]
-            src, dst = (q_.at[stage, xs[j], ts[j]] for j in (0, 1))
+            src, dst = (q_[stage].at[xs[j], ts[j]] for j in (0, 1))
         else:
             xs = {1: (3, 0), -1: (0, 5), 0: (pl.ds(0, 4), pl.ds(1, 4))}[dx]
             ts = {
@@ -122,7 +128,7 @@
                 -1: (pl.ds(0, 8), pl.ds(24, 8)),
                 0: (pl.ds(0, 16), pl.ds(8, 16)),
             }[dt]
-            src, dst = es.at[stage, xs[0], ts[0]], er.at[stage, xs[1], ts[1]]
+            src, dst = es[stage].at[xs[0], ts[0]], er[stage].at[xs[1], ts[1]]
         return pltpu.make_async_remote_copy(
             src_ref=src, dst_ref=dst, send_sem=send_sem.at[stage, i], recv_sem=recv_sem.at[stage, i],
             device_id=to, device_id_type=MESH,
@@ -151,27 +157,28 @@
 
     def spread(stage, xs, update, carry):
         for x in xs:
-            g = er[stage, x] + 2.0 * er[stage, x + 1] + er[stage, x + 2]
+            g = er[stage][x] + 2.0 * er[stage][x + 1] + er[stage][x + 2]
             fs[x] = g
             ff[x] = fs[x, pl.ds(7, 16)] + 2.0 * fs[x, pl.ds(8, 16)] + fs[x, pl.ds(9, 16)]
         need = sorted({x + d for x in xs for d in (0, 1, 2)})
 
-        def step(t, carry):
-            sums = {
-                x: q_[stage, x, t] + 2.0 * q_[stage, x, t + 1] + q_[stage, x, t + 2] for x in need
-            }
-            for x in xs:
-                a = sums[x] + 2.0 * sums[x + 1] + sums[x + 2]
-                smoothed = (
-                    2.0 * a
-                    + jnp.where(row == 0, 0.0, pltpu.roll(a, 1, 0))
-                    + jnp.where(row == 15, 0.0, pltpu.roll(a, 15, 0))
-                    + edge * ff[x, pl.ds(t, 1), :]
-                )
-                carry = update(x, t, smoothed, carry)
+        q = q_[stage]
+
+        def step(i, carry):
+            for t in (UNROLL * i + j for j in range(UNROLL)):
+                sums = {x: q[x, t] + 2.0 * q[x, t + 1] + q[x, t + 2] for x in need}
+                for x in xs:
+                    a = sums[x] + 2.0 * sums[x + 1] + sums[x + 2]
+                    smoothed = (
+                        2.0 * a
+                        + jnp.where(row == 0, 0.0, pltpu.roll(a, 1, 0))
+                        + jnp.where(row == 15, 0.0, pltpu.roll(a, 15, 0))
+                        + edge * ff[x, pl.ds(t, 1), :]
+                    )
+                    carry = update(x, t, smoothed, carry)
             return carry
 
-        return lax.fori_loop(0, 16, step, carry)
+        return lax.fori_loop(0, 16 // UNROLL, step, carry)
 
     def keep_sum(i, total):
         acc[pl.ds(i, 1), :] = jnp.sum(total, axis=0, keepdims=True)
@@ -183,12 +190,13 @@
 
     place(nin, put_n)
 
-    def first(t, carry):
-        for x in range(4):
-            emit(0, x, t, n_[x, t])
+    def first(i, carry):
+        for t in (UNROLL * i + j for j in range(UNROLL)):
+            for x in range(4):
+                emit(0, x, t, n_[x, t])
         return carry
 
-    lax.fori_loop(0, 16, first, 0)
+    lax.fori_loop(0, 16 // UNROLL, first, 0)
     pl.semaphore_wait(barrier, peers - 1)
     send(0, FAR)
     send(0, NEAR)
@@ -312,10 +320,10 @@
         scratch_shapes=[vmem(*shape)] * 3
         + [vmem(8, 8, 16, 128)]
         + [vmem(*whole)] * 9
+        + [vmem(6, 18, 16, 128)] * STAGES
+        + [vmem(4, 16, 128)] * STAGES
+        + [vmem(6, 32, 128)] * STAGES
         + [
-            vmem(STAGES, 6, 18, 16, 128),
-            vmem(STAGES, 4, 16, 128),
-            vmem(STAGES, 6, 32, 128),
             vmem(4, 32, 128),
             vmem(4, 16, 128),
             vmem(8, 128),
@@ -327,7 +335,7 @@
             pltpu.SemaphoreType.DMA,
         ],
         compiler_params=pltpu.CompilerParams(
-            collective_id=0, has_side_effects=True, vmem_limit_bytes=32 * 1024 * 1024
+            collective_id=0, has_side_effects=True, vmem_limit_bytes=60 * 1024 * 1024
         ),
     )(
         brick_slots, brick_counts,

time: 44.3 us -> 39.5 us (0.89)
  local copies, waits for them, and re-layouts: 4.2 us -> 1.67 us
  Pallas kernels: 39.2 us -> 37 us
    unnamed x9 -> x1, local copies, waits for them, and re-layouts: 4.2 us -> 1.67 us
    pallas_call x1, Pallas kernels: 39.2 us -> 37 us  [per_device(): pl.pallas_call(functools.partial(kernel, nx, nt), out_shape=jax.ShapeDtyp...]
where the time goes in v2:
time: 39.5 us; the launch traced here: 39.3 us
  Pallas kernels  37 us (94%)
  local copies, waits for them, and re-layouts  1.67 us (4%)
  between operations  0.66 us (2%)
    pallas_call x1, Pallas kernels, per_device(): pl.pallas_call(functools.partial(kernel, nx, nt), out_shape=jax.ShapeDtyp...  37 us
    unnamed x1, local copies, waits for them, and re-layouts  1.67 us

profile of v2, /device:TPU:0, one launch (start us, length us, event | category | flops | bytes accessed | tf_op | source)
XLA Modules:
  0.0 39.3 jit_solution(15716022057820499361)
XLA Ops:
  0.7 37.0 %shard_map.55 = f32[4,8,16,128]{3,2,1,0:T(8,128)} custom-call(s32[1,1,1,4]{3,2,1,0:T(1,128)} %slots.1, s32[1,1,1]{2,1,0:T(1,128)S(6)} %copy.7.counts, f32[4,8,16,128]{3,2,1,0:T(8,128)} %bitcast.5, f32[4,8,16,128]{3,2,1,0:T(8,128)} %bitcast.6, f32[4,8,16,128]{3,2,1,0:T(8,128)} %bitcast.7), custom_call_target="tpu_custom_call" | custom-call | tf_op jit(solution)/shard_map/pallas_call | solution.py:315
  37.7 1.7 %copy.8 = f32[1,1,1,4,8,8,2,128]{7,6,5,4,3,2,1,0:T(2,128)} copy(f32[1,1,1,4,8,8,2,128]{7,6,5,4,3,2,1,0:T(2,128)} %bitcast.4) | data formatting | bytes 524288

commit v3 on v2

--- a/solution.py
+++ b/solution.py
@@ -10,11 +10,13 @@
 MESH = pl.DeviceIdType.MESH
 SHIFT = 0.5
 STAGES = 4
-UNROLL = 4
+UNROLL = 8
 SIDES = (-1, 0, 1)
 MESSAGES = [(dx, dt, dl) for dl in (0, 1) for dx in SIDES for dt in SIDES if (dx, dt, dl) != (0, 0, 0)]
 NEAR = [m for m in MESSAGES if m[0] == 0]
-FAR = [m for m in MESSAGES if m[0] != 0]
+FACES = [(1, 0, 0), (-1, 0, 0)]
+FAR = FACES + [m for m in MESSAGES if m[0] != 0 and m not in FACES]
+SEND_ORDER = FACES + NEAR + FAR[2:]
 
 
 def kernel(
@@ -198,8 +200,7 @@
 
     lax.fori_loop(0, 16 // UNROLL, first, 0)
     pl.semaphore_wait(barrier, peers - 1)
-    send(0, FAR)
-    send(0, NEAR)
+    send(0, SEND_ORDER)
 
     loads[1].wait()
     loads[2].wait()
@@ -256,8 +257,7 @@
         receive(stage, FAR)
         carry = spread(stage, (0, 3), update, carry)
         if stage + 1 < STAGES:
-            send(stage + 1, FAR)
-            send(stage + 1, NEAR)
+            send(stage + 1, SEND_ORDER)
         for total in carry:
             keep_sum(rows, total)
             rows += 1

time: 39.5 us -> 39.2 us (level)
  no operation moved by 1% of the time
where the time goes in v3:
time: 39.2 us; the launch traced here: 39 us
  Pallas kernels  36.7 us (94%)
  local copies, waits for them, and re-layouts  1.67 us (4%)
  between operations  0.66 us (2%)
    pallas_call x1, Pallas kernels, per_device(): pl.pallas_call(functools.partial(kernel, nx, nt), out_shape=jax.ShapeDtyp...  36.7 us
    unnamed x1, local copies, waits for them, and re-layouts  1.67 us

profile of v3, /device:TPU:0, one launch (start us, length us, event | category | flops | bytes accessed | tf_op | source)
XLA Modules:
  0.0 39.0 jit_solution(441560260989540213)
XLA Ops:
  0.7 36.7 %shard_map.55 = f32[4,8,16,128]{3,2,1,0:T(8,128)} custom-call(s32[1,1,1,4]{3,2,1,0:T(1,128)} %slots.1, s32[1,1,1]{2,1,0:T(1,128)S(6)} %copy.7.counts, f32[4,8,16,128]{3,2,1,0:T(8,128)} %bitcast.5, f32[4,8,16,128]{3,2,1,0:T(8,128)} %bitcast.6, f32[4,8,16,128]{3,2,1,0:T(8,128)} %bitcast.7), custom_call_target="tpu_custom_call" | custom-call | tf_op jit(solution)/shard_map/pallas_call | solution.py:315
  37.3 1.7 %copy.8 = f32[1,1,1,4,8,8,2,128]{7,6,5,4,3,2,1,0:T(2,128)} copy(f32[1,1,1,4,8,8,2,128]{7,6,5,4,3,2,1,0:T(2,128)} %bitcast.4) | data formatting | bytes 524288

commit v4 on v3

--- a/solution.py
+++ b/solution.py
@@ -14,9 +14,8 @@
 SIDES = (-1, 0, 1)
 MESSAGES = [(dx, dt, dl) for dl in (0, 1) for dx in SIDES for dt in SIDES if (dx, dt, dl) != (0, 0, 0)]
 NEAR = [m for m in MESSAGES if m[0] == 0]
-FACES = [(1, 0, 0), (-1, 0, 0)]
-FAR = FACES + [m for m in MESSAGES if m[0] != 0 and m not in FACES]
-SEND_ORDER = FACES + NEAR + FAR[2:]
+FAR = [m for m in MESSAGES if m[0] != 0]
+SEND_ORDER = sorted(MESSAGES, key=lambda m: -abs(m[0]) - abs(m[1]) - m[2])
 
 
 def kernel(

time: 39.2 us -> 36.2 us (0.923)
  Pallas kernels: 36.7 us -> 33.7 us
    pallas_call x1, Pallas kernels: 36.7 us -> 33.7 us  [per_device(): pl.pallas_call(functools.partial(kernel, nx, nt), out_shape=jax.ShapeDtyp...]
where the time goes in v4:
time: 36.2 us; the launch traced here: 36 us
  Pallas kernels  33.7 us (93%)
  local copies, waits for them, and re-layouts  1.67 us (5%)
  between operations  0.66 us (2%)
    pallas_call x1, Pallas kernels, per_device(): pl.pallas_call(functools.partial(kernel, nx, nt), out_shape=jax.ShapeDtyp...  33.7 us
    unnamed x1, local copies, waits for them, and re-layouts  1.67 us

profile of v4, /device:TPU:0, one launch (start us, length us, event | category | flops | bytes accessed | tf_op | source)
XLA Modules:
  0.0 36.0 jit_solution(10350905654512606127)
XLA Ops:
  0.7 33.7 %shard_map.55 = f32[4,8,16,128]{3,2,1,0:T(8,128)} custom-call(s32[1,1,1,4]{3,2,1,0:T(1,128)} %slots.1, s32[1,1,1]{2,1,0:T(1,128)S(6)} %copy.7.counts, f32[4,8,16,128]{3,2,1,0:T(8,128)} %bitcast.5, f32[4,8,16,128]{3,2,1,0:T(8,128)} %bitcast.6, f32[4,8,16,128]{3,2,1,0:T(8,128)} %bitcast.7), custom_call_target="tpu_custom_call" | custom-call | tf_op jit(solution)/shard_map/pallas_call | solution.py:314
  34.4 1.7 %copy.8 = f32[1,1,1,4,8,8,2,128]{7,6,5,4,3,2,1,0:T(2,128)} copy(f32[1,1,1,4,8,8,2,128]{7,6,5,4,3,2,1,0:T(2,128)} %bitcast.4) | data formatting | bytes 524288

commit v5 on v4

--- a/solution.py
+++ b/solution.py
@@ -253,10 +253,14 @@
     for stage, (update, count) in enumerate(((update0, 1), (update1, 2), (update2, 3), (update3, 1))):
         receive(stage, NEAR)
         carry = spread(stage, (1, 2), update, (zero,) * count)
-        receive(stage, FAR)
-        carry = spread(stage, (0, 3), update, carry)
-        if stage + 1 < STAGES:
-            send(stage + 1, SEND_ORDER)
+        rest = SEND_ORDER
+        for x, way in ((3, 1), (0, -1)) if stage % 2 else ((0, -1), (3, 1)):
+            receive(stage, [m for m in FAR if m[0] == -way])
+            carry = spread(stage, (x,), update, carry)
+            if stage + 1 < STAGES:
+                ready = [m for m in rest if m[0] == way or x == 3 * (1 - stage % 2)]
+                send(stage + 1, ready)
+                rest = [m for m in rest if m not in ready]
         for total in carry:
             keep_sum(rows, total)
             rows += 1

time: 36.2 us -> 36.2 us (level)
  no operation moved by 1% of the time
where the time goes in v5:
time: 36.2 us; the launch traced here: 36.1 us
  Pallas kernels  33.7 us (93%)
  local copies, waits for them, and re-layouts  1.67 us (5%)
  between operations  0.66 us (2%)
    pallas_call x1, Pallas kernels, per_device(): pl.pallas_call(functools.partial(kernel, nx, nt), out_shape=jax.ShapeDtyp...  33.7 us
    unnamed x1, local copies, waits for them, and re-layouts  1.67 us

profile of v5, /device:TPU:0, one launch (start us, length us, event | category | flops | bytes accessed | tf_op | source)
XLA Modules:
  0.0 36.1 jit_solution(17869203171488543678)
XLA Ops:
  0.7 33.7 %shard_map.55 = f32[4,8,16,128]{3,2,1,0:T(8,128)} custom-call(s32[1,1,1,4]{3,2,1,0:T(1,128)} %slots.1, s32[1,1,1]{2,1,0:T(1,128)S(6)} %copy.7.counts, f32[4,8,16,128]{3,2,1,0:T(8,128)} %bitcast.5, f32[4,8,16,128]{3,2,1,0:T(8,128)} %bitcast.6, f32[4,8,16,128]{3,2,1,0:T(8,128)} %bitcast.7), custom_call_target="tpu_custom_call" | custom-call | tf_op jit(solution)/shard_map/pallas_call | solution.py:318
  34.4 1.7 %copy.8 = f32[1,1,1,4,8,8,2,128]{7,6,5,4,3,2,1,0:T(2,128)} copy(f32[1,1,1,4,8,8,2,128]{7,6,5,4,3,2,1,0:T(2,128)} %bitcast.4) | data formatting | bytes 524288
